TPU v7x, 32 devices: a whole 2x2x4 slice. The times are simulated.
32 devices in a mesh: band: 4 (over y, x), pw: 8 (over z, core).
Axes of the slice: x: 2, y: 2, z: 4, core: 2. Of those that a mesh axis runs over, the one named last changes fastest.
Arguments:
- psi: float32 [2, 8, 16384], P(None, None, 'pw'), may hold values from -60 to 60
- energies: float32 [8], P('band'), may hold values from -2 to 0
- kinetic: float32 [16384], P('pw'), may hold values from 0.05 to 20
- vloc: float32 [128, 128, 128], P('pw'), may hold values from 0.5 to 2
- dv: float32 [128, 128, 128], P('pw'), may hold values from -5 to 5
- beta: float32 [2, 64, 16384], P(None, None, 'pw'), may hold values from -0.046875 to 0.046875
- nl_diag: float32 [64], replicated, may hold values from 1 to 10
- nl_coupling: float32 [64], replicated, may hold values from -4 to 4
- proj_counts: int32 [16], replicated, may hold values from 1 to 13, 64 in all
- pw_map: int32 [16384], P('pw'), may hold values from 0 to 16383, as said below
- stick_pos: int32 [1024], replicated, may hold values from 0 to 16383, as said below
Outputs:
- dpsi: float32 [2, 8, 16384], P(None, 'band', 'pw')
- residual: float32 [2, 8, 16384], P(None, 'band', 'pw')
- drho: float32 [128, 128, 128], P('pw', 'band')
Inputs may be any that keep to these rules, and one draw needn't show every extreme that they name: `pw_map`: within each block of 2048 entries (the plane waves of one pw index) the values are distinct, and each block holds 0 and 16383. `stick_pos`: all values distinct; 0 and 16383 appear.
All inputs are finite; a program needn't handle non-finite values.
Results may differ from a plain program's by a relative error of at most 0.0003.
Values sent between devices are 32-bit elements; how exact they have to be, the bound alone decides.
A program may use at most 256 MiB of HBM per device.

v0:
```python
import math
import jax
import jax.numpy as jnp
from jax import lax
from jax.sharding import PartitionSpec as P

ITERS = 2
PRECISE = lax.Precision.HIGHEST
ALPHA_SHIFT = 4.0


def dft_tables(length):
    positions = jnp.arange(length, dtype=jnp.int32)
    phases = positions[:, None] * positions[None, :] % length
    angles = phases.astype(jnp.float32) * (2.0 * math.pi / length)
    return (jnp.cos(angles), jnp.sin(angles))


def complex_transform(values_in, tables, direction_sign, einsum_form):
    cosine_table, sine_table = tables
    real_part, imag_part = (values_in[0], values_in[1])

    def product(table, operand):
        return jnp.einsum(einsum_form, table, operand, precision=PRECISE)

    return jnp.stack(
        [
            product(cosine_table, real_part) - direction_sign * product(sine_table, imag_part),
            product(cosine_table, imag_part) + direction_sign * product(sine_table, real_part),
        ]
    )


def project_onto(basis, vector):

    def product(left, right):
        return jnp.einsum("kg,ng->kn", left, right, precision=PRECISE)

    return jnp.stack(
        [
            product(basis[0], vector[0]) + product(basis[1], vector[1]),
            product(basis[0], vector[1]) - product(basis[1], vector[0]),
        ]
    )


def expand(basis, weights):

    def product(left, right):
        return jnp.einsum("kn,kg->ng", left, right, precision=PRECISE)

    return jnp.stack(
        [
            product(weights[0], basis[0]) - product(weights[1], basis[1]),
            product(weights[0], basis[1]) + product(weights[1], basis[0]),
        ]
    )


def dot_bands(left, right):
    return jnp.sum(left * right, axis=(0, 2))


def shards(
    psi, energies, kinetic, vloc, dv, beta, nl_diag, nl_coupling, proj_counts, pw_map, stick_pos
):
    grid_size = vloc.shape[1]
    plane_count = vloc.shape[0]
    columns = stick_pos.shape[0] // lax.axis_size("pw")
    total_pw = kinetic.shape[0] * lax.axis_size("pw")
    block_bands = energies.shape[0]
    norm_scale = 1.0 / math.sqrt(grid_size**3)
    tables = dft_tables(grid_size)
    own_states = lax.dynamic_slice_in_dim(psi, lax.axis_index("band") * block_bands, block_bands, 1)
    block_ends = jnp.cumsum(proj_counts)
    proj_index = jnp.arange(beta.shape[1], dtype=jnp.int32)
    atom_of = jnp.sum((proj_index[:, None] >= block_ends[None, :]).astype(jnp.int32), axis=1)
    same_atom = (atom_of[:, None] == atom_of[None, :]).astype(jnp.float32)

    def to_sticks(coeffs):
        item_count = coeffs.shape[1]
        flat_grid = (
            jnp.zeros((2, item_count, grid_size * columns), jnp.float32)
            .at[:, :, pw_map]
            .set(coeffs)
        )
        sticks = flat_grid.reshape(2, item_count, grid_size, columns)
        return complex_transform(sticks, tables, 1.0, "zk,bks->bzs")

    def planes_inverse(received):
        item_count = received.shape[1]
        flat_grid = jnp.zeros((2, item_count, plane_count, grid_size * grid_size), jnp.float32)
        flat_grid = flat_grid.at[:, :, :, stick_pos].set(received)
        field = flat_grid.reshape(2, item_count, plane_count, grid_size, grid_size)
        field = complex_transform(field, tables, 1.0, "yk,bpkx->bpyx")
        field = complex_transform(field, tables, 1.0, "xk,bpyk->bpyx")
        return field * norm_scale

    def planes_forward(field):
        item_count = field.shape[1]
        spectrum = complex_transform(field, tables, -1.0, "yk,bpkx->bpyx")
        spectrum = complex_transform(spectrum, tables, -1.0, "xk,bpyk->bpyx")
        spectrum = spectrum.reshape(2, item_count, plane_count, grid_size * grid_size)
        return jnp.take(spectrum, stick_pos, axis=3)

    def with_potential(potential):

        def apply_field(received):
            field = planes_inverse(received)
            return (field, planes_forward(field * potential))

        return apply_field

    def real_space(coeffs, plane_fn):
        return plane_fn(
            lax.all_to_all(to_sticks(coeffs), "pw", split_axis=2, concat_axis=3, tiled=True)
        )

    def from_sticks(back_values):
        sticks = lax.all_to_all(back_values, "pw", split_axis=3, concat_axis=2, tiled=True)
        item_count = sticks.shape[1]
        spectrum = complex_transform(sticks, tables, -1.0, "zk,bks->bzs") * norm_scale
        spectrum = spectrum.reshape(2, item_count, grid_size * columns)
        return jnp.take(spectrum, pw_map, axis=2)

    def projections(vector):
        return lax.psum((project_onto(psi, vector), project_onto(beta, vector)), "pw")

    def preconditioned_norm(residual, precond_res):
        return lax.psum(dot_bands(residual, precond_res), "pw")

    diagonal_shift = kinetic[None, None, :] - energies[None, :, None]
    precond = 1.0 / (1.0 + diagonal_shift)
    state_planes, dv_back = real_space(own_states, with_potential(dv))
    dvpsi = from_sticks(dv_back)
    rhs_state, rhs_beta = projections(dvpsi)
    rhs = -(dvpsi - expand(psi, rhs_state) / total_pw)
    solution = jnp.zeros_like(rhs)
    residual = rhs
    search = precond * residual
    norm_now = preconditioned_norm(residual, search)
    for iteration in range(ITERS):
        search_planes, local_back = real_space(search, with_potential(vloc))
        local_part = from_sticks(local_back)
        state_proj, beta_proj = projections(search)
        weighted = nl_coupling[None, :, None] * beta_proj
        grouped = jnp.einsum("ij,cjn->cin", same_atom, weighted, precision=PRECISE)
        nonlocal_part = expand(
            beta, nl_diag[None, :, None] * beta_proj + nl_coupling[None, :, None] * grouped
        )
        occupied_part = ALPHA_SHIFT / total_pw * expand(psi, state_proj)
        image = diagonal_shift * search + local_part + nonlocal_part + occupied_part
        step_len = norm_now / lax.psum(dot_bands(search, image), "pw")
        solution = solution + step_len[None, :, None] * search
        residual = residual - step_len[None, :, None] * image
        if iteration + 1 < ITERS:
            precond_res = precond * residual
            norm_next = preconditioned_norm(residual, precond_res)
            ratio = norm_next / norm_now
            search = precond_res + ratio[None, :, None] * search
            norm_now = norm_next
    solution_planes = real_space(solution, planes_inverse)
    density_scale = 2.0 * grid_size**3 / total_pw
    density_term = density_scale * jnp.sum(state_planes * solution_planes, axis=(0, 1))
    drho = lax.psum_scatter(density_term, "band", scatter_dimension=1, tiled=True)
    return (solution, residual, drho)


def solution(mesh):
    placed = (
        P(None, None, "pw"),
        P("band"),
        P("pw"),
        P("pw", None, None),
        P("pw", None, None),
        P(None, None, "pw"),
        P(),
        P(),
        P(),
        P("pw"),
        P(),
    )
    return jax.shard_map(
        shards,
        mesh=mesh,
        in_specs=placed,
        out_specs=(P(None, "band", "pw"), P(None, "band", "pw"), P("pw", "band", None)),
        check_vma=False,
    )
```

profile of v0, /device:TPU:0, one launch (start us, length us, event | category | flops | bytes accessed | tf_op | source)
XLA Modules:
  0.0 2317.2 jit_solution(12426958503764950152)
XLA Ops:
  15.2 186.4 %scatter_fusion = f32[2,2,16384]{1,0,2:T(2,128)} fusion(f32[2,2,16384]{1,0,2:T(2,128)} %broadcast.134.clone, s32[2048]{0:T(1024)S(1)} %get-tuple-element.45, f32[2048,2,2]{2,1,0:T(2,128)S(1)} %copy.624), kind=kCustom, calls=%fused_computation.6 | custom fusion | bytes 106496 | tf_op jit(solution)/shard_map/scatter | solution.py:85
  201.6 19.3 fusion.792
  263.6 93.6 %scatter_fusion.1 = f32[2,2,16,16384]{2,1,3,0:T(2,128)} fusion(f32[2,2,16,16384]{2,1,3,0:T(2,128)} %broadcast.131.clone, s32[1024]{0:T(1024)S(1)} %get-tuple-element.47, f32[1024,2,2,16]{3,2,1,0:T(2,128)S(1)} %copy.634), kind=kCustom, calls=%fused_computation.7 | custom fusion | bytes 790528 | tf_op jit(solution)/shard_map/scatter | solution.py:93
  357.2 23.1 fusion.788
  482.9 36.1 %copy.653 = f32[2,2,16,16384]{2,1,3,0:T(2,128)} copy(f32[2,2,16,16384]{3,2,1,0:T(8,128)} %pad_maximum_fusion.1) | data formatting | bytes 8388608 | tf_op jit(solution)/shard_map/stack | solution.py:26
  519.0 17.8 gather_fusion
  621.9 186.4 %scatter_fusion.2 = f32[2,2,16384]{1,0,2:T(2,128)} fusion(f32[2,2,16384]{1,0,2:T(2,128)} %broadcast.134.clone.1, s32[2048]{0:T(1024)S(1)} %get-tuple-element.45, f32[2048,2,2]{2,1,0:T(2,128)S(1)} %copy.663), kind=kCustom, calls=%fused_computation.8 | custom fusion | bytes 106496 | tf_op jit(solution)/shard_map/scatter | solution.py:85
  808.3 19.3 fusion.791
  879.4 93.6 %scatter_fusion.3 = f32[2,2,16,16384]{2,1,3,0:T(2,128)} fusion(f32[2,2,16,16384]{2,1,3,0:T(2,128)} %broadcast.131.clone.1, s32[1024]{0:T(1024)S(1)} %get-tuple-element.47, f32[1024,2,2,16]{3,2,1,0:T(2,128)S(1)} %copy.673), kind=kCustom, calls=%fused_computation.9 | custom fusion | bytes 790528 | tf_op jit(solution)/shard_map/scatter | solution.py:93
  972.9 23.1 fusion.787
  1098.3 36.1 %copy.692 = f32[2,2,16,16384]{2,1,3,0:T(2,128)} copy(f32[2,2,16,16384]{3,2,1,0:T(8,128)} %pad_maximum_fusion.2) | data formatting | bytes 8388608 | tf_op jit(solution)/shard_map/stack | solution.py:26
  1134.5 17.8 gather_fusion.2
  1252.1 186.4 %scatter_fusion.4 = f32[2,2,16384]{1,0,2:T(2,128)} fusion(f32[2,2,16384]{1,0,2:T(2,128)} %broadcast.134.clone.2, s32[2048]{0:T(1024)S(1)} %get-tuple-element.45, f32[2048,2,2]{2,1,0:T(2,128)S(1)} %copy.703), kind=kCustom, calls=%fused_computation.10 | custom fusion | bytes 106496 | tf_op jit(solution)/shard_map/scatter | solution.py:85
  1438.5 19.3 fusion.790
  1476.3 17.4 all-reduce
  1509.7 93.6 %scatter_fusion.5 = f32[2,2,16,16384]{2,1,3,0:T(2,128)} fusion(f32[2,2,16,16384]{2,1,3,0:T(2,128)} %broadcast.131.clone.2, s32[1024]{0:T(1024)S(1)} %get-tuple-element.47, f32[1024,2,2,16]{3,2,1,0:T(2,128)S(1)} %copy.713), kind=kCustom, calls=%fused_computation.11 | custom fusion | bytes 790528 | tf_op jit(solution)/shard_map/scatter | solution.py:93
  1603.3 23.1 fusion.786
  1728.7 36.1 %copy.732 = f32[2,2,16,16384]{2,1,3,0:T(2,128)} copy(f32[2,2,16,16384]{3,2,1,0:T(8,128)} %pad_maximum_fusion.3) | data formatting | bytes 8388608 | tf_op jit(solution)/shard_map/stack | solution.py:26
  1764.8 17.8 gather_fusion.4
  1863.7 186.4 %scatter_fusion.6 = f32[2,2,16384]{1,0,2:T(2,128)} fusion(f32[2,2,16384]{1,0,2:T(2,128)} %broadcast.134, s32[2048]{0:T(1024)S(1)} %get-tuple-element.45, f32[2048,2,2]{2,1,0:T(2,128)S(1)} %copy.742), kind=kCustom, calls=%fused_computation.12 | custom fusion | bytes 106496 | tf_op jit(solution)/shard_map/scatter | solution.py:85
  2050.1 19.3 fusion.789
  2106.8 93.6 %scatter_fusion.7 = f32[2,2,16,16384]{2,1,3,0:T(2,128)} fusion(f32[2,2,16,16384]{2,1,3,0:T(2,128)} %broadcast.131, s32[1024]{0:T(1024)S(1)} %get-tuple-element.47, f32[1024,2,2,16]{3,2,1,0:T(2,128)S(1)} %copy.752), kind=kCustom, calls=%fused_computation.13 | custom fusion | bytes 790528 | tf_op jit(solution)/shard_map/scatter | solution.py:93
  2200.4 23.1 fusion.785
  2283.1 26.8 %reduce-scatter.2.cloned.1.call-done = f32[16,32,128]{2,1,0:T(8,128)} async-done(((f32[16,128,128]{2,1,0:T(8,128)}), f32[16,32,128]{2,1,0:T(8,128)}) %reduce-scatter.2.cloned.1.call-update) | async-done | bytes 262160 | tf_op jit(solution)/shard_map/reduce_scatter | solution.py:165
  (344 shorter events, 805.8 us)
Async XLA Ops:
  231.9 9.6 copy-start.27
  231.9 9.6 copy-start.23
  233.0 8.6 copy-start.29
  233.0 8.8 copy-start.24
  234.5 16.7 all-to-all-start
  393.5 4.9 copy-start.2
  433.6 4.0 copy-start.10
  542.1 7.4 copy-start.28
  542.1 7.4 copy-start.30
  545.7 13.3 all-to-all-start.1
  582.7 13.6 copy-start.1
  582.7 31.0 %copy-start = (f32[2,64,2048]{2,1,0:T(8,128)S(1)}, f32[2,64,2048]{2,1,0:T(8,128)}, u32[]{:S(2)}) copy-start(f32[2,64,2048]{2,1,0:T(8,128)} %param.20) | copy-start | bytes 3145732
  838.6 24.8 %copy-start.31 = (f32[64]{0:T(128)S(1)}, f32[64]{0:T(128)}, u32[]{:S(2)}) copy-start(f32[64]{0:T(128)} %param.22) | copy-start | bytes 772
  838.6 24.8 %copy-start.32 = (f32[64]{0:T(128)S(1)}, f32[64]{0:T(128)}, u32[]{:S(2)}) copy-start(f32[64]{0:T(128)} %param.21) | copy-start | bytes 772
  841.1 23.8 %all-to-all-start.2 = ((f32[2,2,128,128]{3,1,0,2:T(2,128)}), f32[2,2,128,128]{3,1,0,2:T(2,128)S(1)}, u32[]{:S(2)}, u32[]{:S(2)}) async-start(f32[2,2,128,128]{3,1,0,2:T(2,128)} %copy.670), calls=%async_computation.2 | async-start | bytes 524288 | tf_op jit(solution)/shard_map/all_to_all | solution.py:116
  1009.2 4.9 copy-start.4
  1038.4 4.0 copy-start.17
  1161.1 13.2 all-to-all-start.3
  1471.3 23.9 %all-to-all-start.4 = ((f32[2,2,128,128]{3,1,0,2:T(2,128)}), f32[2,2,128,128]{3,1,0,2:T(2,128)S(1)}, u32[]{:S(2)}, u32[]{:S(2)}) async-start(f32[2,2,128,128]{3,1,0,2:T(2,128)} %copy.710), calls=%async_computation.4 | async-start | bytes 524288 | tf_op jit(solution)/shard_map/all_to_all | solution.py:116
  1639.6 4.9 copy-start.6
  1791.4 13.1 all-to-all-start.5
  1794.9 515.0 %reduce-scatter.2.cloned.1.call-start = ((), (), s32[]{:S(2)}) async-start(), calls=%async_computation.8 | async-start | bytes 1310720 | tf_op jit(solution)/shard_map/reduce_scatter | solution.py:165
  1856.6 7.1 copy-start.25
  2236.7 4.9 copy-start.8
  (16 other events, 53.6 us)
Sparse Core Ops, SparseCore 0:
  2283.2 26.6 reduce-scatter.1
where the time goes:
time: 2350 us; the launch traced here: 2320 us
  local copies, waits for them, and re-layouts  1820 us (77%)
  matrix products  254 us (11%)
  blocking collectives  105 us (4%)
  waiting for transfers between devices  61.5 us (3%)
  other arithmetic  39.9 us (2%)
  starting transfers between devices  24.9 us (1%)
    scatter x4, local copies, waits for them, and re-layouts, to_sticks(): flat_grid = jnp.zeros((2, item_count, grid_size * columns), jnp.float32)....  746 us
    scatter x4, local copies, waits for them, and re-layouts, planes_inverse(): flat_grid = flat_grid.at[:, :, :, stick_pos].set(received)  374 us
    dot_general x84, matrix products, product(): return jnp.einsum(einsum_form, table, operand, precision=PRECISE)  241 us
    slice x11, local copies, waits for them, and re-layouts, complex_transform(): real_part, imag_part = (values_in[0], values_in[1])  170 us
    squeeze x16, local copies, waits for them, and re-layouts, complex_transform(): real_part, imag_part = (values_in[0], values_in[1])  148 us
    another operation x19, local copies, waits for them, and re-layouts, complex_transform(): jnp.stack([product(cosine_table, real_part) - direction_sign * product(si...  128 us
    another operation x9, local copies, waits for them, and re-layouts  68.1 us
    gather x3, local copies, waits for them, and re-layouts, planes_forward(): return jnp.take(spectrum, stick_pos, axis=3)  53.4 us
  transfers between devices with their start and end apart: 7, of which 5 were waited for; matrix products, arithmetic and copies ran while one was open for 0% of the time, Pallas kernels for 0%

commit v1 on v0

--- a/solution.py
+++ b/solution.py
@@ -117,7 +117,12 @@
         )
 
     def from_sticks(back_values):
-        sticks = lax.all_to_all(back_values, "pw", split_axis=3, concat_axis=2, tiled=True)
+        sticks = jnp.concatenate(
+            lax.all_to_all(
+                jnp.stack(jnp.split(back_values, lax.axis_size("pw"), axis=3)), "pw", 0, 0
+            ),
+            axis=2,
+        )
         item_count = sticks.shape[1]
         spectrum = complex_transform(sticks, tables, -1.0, "zk,bks->bzs") * norm_scale
         spectrum = spectrum.reshape(2, item_count, grid_size * columns)

time: 2350 us -> 2320 us (0.987)
    another operation x9 -> x39, local copies, waits for them, and re-layouts: 68.1 us -> 76.1 us
where the time goes in v1:
time: 2320 us; the launch traced here: 2290 us
  local copies, waits for them, and re-layouts  1800 us (78%)
  matrix products  254 us (11%)
  blocking collectives  104 us (4%)
  waiting for transfers between devices  61.7 us (3%)
  other arithmetic  30.8 us (1%)
  starting transfers between devices  23.8 us (1%)
    scatter x4, local copies, waits for them, and re-layouts, to_sticks(): flat_grid = jnp.zeros((2, item_count, grid_size * columns), jnp.float32)....  748 us
    scatter x4, local copies, waits for them, and re-layouts, planes_inverse(): flat_grid = flat_grid.at[:, :, :, stick_pos].set(received)  375 us
    dot_general x84, matrix products, product(): return jnp.einsum(einsum_form, table, operand, precision=PRECISE)  241 us
    slice x11, local copies, waits for them, and re-layouts, complex_transform(): real_part, imag_part = (values_in[0], values_in[1])  170 us
    squeeze x16, local copies, waits for them, and re-layouts, complex_transform(): real_part, imag_part = (values_in[0], values_in[1])  148 us
    another operation x19, local copies, waits for them, and re-layouts, complex_transform(): jnp.stack([product(cosine_table, real_part) - direction_sign * product(si...  129 us
    another operation x9, local copies, waits for them, and re-layouts  68.2 us
    psum x3, blocking collectives, projections(): lax.psum((project_onto(psi, vector), project_onto(beta, vector)), 'pw')  49.3 us
  transfers between devices with their start and end apart: 7, of which 5 were waited for; matrix products, arithmetic and copies ran while one was open for 0% of the time, Pallas kernels for 0%

profile of v1, /device:TPU:0, one launch (start us, length us, event | category | flops | bytes accessed | tf_op | source)
XLA Modules:
  0.0 2289.3 jit_solution(778797705320769484)
XLA Ops:
  15.3 186.9 %scatter_fusion = f32[2,2,16384]{1,0,2:T(2,128)} fusion(f32[2,2,16384]{1,0,2:T(2,128)} %broadcast.134.clone, s32[2048]{0:T(1024)S(1)} %get-tuple-element.69, f32[2048,2,2]{2,1,0:T(2,128)S(1)} %copy.681), kind=kCustom, calls=%fused_computation.6 | custom fusion | bytes 106496 | tf_op jit(solution)/shard_map/scatter | solution.py:85
  202.2 19.3 fusion.792
  263.1 93.7 %scatter_fusion.1 = f32[2,2,16,16384]{2,1,3,0:T(2,128)} fusion(f32[2,2,16,16384]{2,1,3,0:T(2,128)} %broadcast.131.clone, s32[1024]{0:T(1024)S(1)} %get-tuple-element.71, f32[1024,2,2,16]{3,2,1,0:T(2,128)S(1)} %copy.691), kind=kCustom, calls=%fused_computation.7 | custom fusion | bytes 790528 | tf_op jit(solution)/shard_map/scatter | solution.py:93
  356.8 23.1 %fusion.788 = (f32[1,2,16,16384]{2,1,3,0:T(2,128)}, f32[1,2,16,16384]{2,1,3,0:T(2,128)}) fusion(f32[2,2,16,16384]{2,1,3,0:T(2,128)} %scatter_fusion.1), kind=kLoop, calls=%fused_computation.890 | loop fusion | bytes 8388608 | tf_op jit(solution)/shard_map/slice | solution.py:21
  482.6 36.2 %copy.710 = f32[2,2,16,16384]{2,1,3,0:T(2,128)} copy(f32[2,2,16,16384]{3,2,1,0:T(8,128)} %pad_maximum_fusion.1) | data formatting | bytes 8388608 | tf_op jit(solution)/shard_map/stack | solution.py:26
  559.0 14.8 copy.726
  612.6 186.9 %scatter_fusion.2 = f32[2,2,16384]{1,0,2:T(2,128)} fusion(f32[2,2,16384]{1,0,2:T(2,128)} %broadcast.134.clone.1, s32[2048]{0:T(1024)S(1)} %get-tuple-element.69, f32[2048,2,2]{2,1,0:T(2,128)S(1)} %copy.728), kind=kCustom, calls=%fused_computation.8 | custom fusion | bytes 106496 | tf_op jit(solution)/shard_map/scatter | solution.py:85
  799.5 19.3 fusion.791
  837.4 17.3 all-reduce.2
  870.6 93.7 %scatter_fusion.3 = f32[2,2,16,16384]{2,1,3,0:T(2,128)} fusion(f32[2,2,16,16384]{2,1,3,0:T(2,128)} %broadcast.131.clone.1, s32[1024]{0:T(1024)S(1)} %get-tuple-element.71, f32[1024,2,2,16]{3,2,1,0:T(2,128)S(1)} %copy.738), kind=kCustom, calls=%fused_computation.9 | custom fusion | bytes 790528 | tf_op jit(solution)/shard_map/scatter | solution.py:93
  964.3 23.1 %fusion.787 = (f32[1,2,16,16384]{2,1,3,0:T(2,128)}, f32[1,2,16,16384]{2,1,3,0:T(2,128)}) fusion(f32[2,2,16,16384]{2,1,3,0:T(2,128)} %scatter_fusion.3), kind=kLoop, calls=%fused_computation.889 | loop fusion | bytes 8388608 | tf_op jit(solution)/shard_map/slice | solution.py:21
  1089.6 36.2 %copy.757 = f32[2,2,16,16384]{2,1,3,0:T(2,128)} copy(f32[2,2,16,16384]{3,2,1,0:T(8,128)} %pad_maximum_fusion.2) | data formatting | bytes 8388608 | tf_op jit(solution)/shard_map/stack | solution.py:26
  1165.6 14.8 copy.773
  1231.3 186.9 %scatter_fusion.4 = f32[2,2,16384]{1,0,2:T(2,128)} fusion(f32[2,2,16384]{1,0,2:T(2,128)} %broadcast.134.clone.2, s32[2048]{0:T(1024)S(1)} %get-tuple-element.69, f32[2048,2,2]{2,1,0:T(2,128)S(1)} %copy.776), kind=kCustom, calls=%fused_computation.10 | custom fusion | bytes 106496 | tf_op jit(solution)/shard_map/scatter | solution.py:85
  1418.2 19.3 fusion.790
  1456.1 17.5 all-reduce
  1489.6 93.7 %scatter_fusion.5 = f32[2,2,16,16384]{2,1,3,0:T(2,128)} fusion(f32[2,2,16,16384]{2,1,3,0:T(2,128)} %broadcast.131.clone.2, s32[1024]{0:T(1024)S(1)} %get-tuple-element.71, f32[1024,2,2,16]{3,2,1,0:T(2,128)S(1)} %copy.786), kind=kCustom, calls=%fused_computation.11 | custom fusion | bytes 790528 | tf_op jit(solution)/shard_map/scatter | solution.py:93
  1583.3 23.1 %fusion.786 = (f32[1,2,16,16384]{2,1,3,0:T(2,128)}, f32[1,2,16,16384]{2,1,3,0:T(2,128)}) fusion(f32[2,2,16,16384]{2,1,3,0:T(2,128)} %scatter_fusion.5), kind=kLoop, calls=%fused_computation.888 | loop fusion | bytes 8388608 | tf_op jit(solution)/shard_map/slice | solution.py:21
  1708.3 36.2 %copy.805 = f32[2,2,16,16384]{2,1,3,0:T(2,128)} copy(f32[2,2,16,16384]{3,2,1,0:T(8,128)} %pad_maximum_fusion.3) | data formatting | bytes 8388608 | tf_op jit(solution)/shard_map/stack | solution.py:26
  1835.0 186.9 %scatter_fusion.6 = f32[2,2,16384]{1,0,2:T(2,128)} fusion(f32[2,2,16384]{1,0,2:T(2,128)} %broadcast.134, s32[2048]{0:T(1024)S(1)} %get-tuple-element.69, f32[2048,2,2]{2,1,0:T(2,128)S(1)} %copy.823), kind=kCustom, calls=%fused_computation.12 | custom fusion | bytes 106496 | tf_op jit(solution)/shard_map/scatter | solution.py:85
  2022.0 19.3 fusion.789
  2078.7 93.7 %scatter_fusion.7 = f32[2,2,16,16384]{2,1,3,0:T(2,128)} fusion(f32[2,2,16,16384]{2,1,3,0:T(2,128)} %broadcast.131, s32[1024]{0:T(1024)S(1)} %get-tuple-element.71, f32[1024,2,2,16]{3,2,1,0:T(2,128)S(1)} %copy.833), kind=kCustom, calls=%fused_computation.13 | custom fusion | bytes 790528 | tf_op jit(solution)/shard_map/scatter | solution.py:93
  2172.4 23.1 %fusion.785 = (f32[1,2,16,16384]{2,1,3,0:T(2,128)}, f32[1,2,16,16384]{2,1,3,0:T(2,128)}) fusion(f32[2,2,16,16384]{2,1,3,0:T(2,128)} %scatter_fusion.7), kind=kLoop, calls=%fused_computation.887 | loop fusion | bytes 8388608 | tf_op jit(solution)/shard_map/slice | solution.py:21
  2255.4 26.8 %reduce-scatter.2.cloned.1.call-done = f32[16,32,128]{2,1,0:T(8,128)} async-done(((f32[16,128,128]{2,1,0:T(8,128)}), f32[16,32,128]{2,1,0:T(8,128)}) %reduce-scatter.2.cloned.1.call-update) | async-done | bytes 262160 | tf_op jit(solution)/shard_map/reduce_scatter | solution.py:170
  (385 shorter events, 781.5 us)
Async XLA Ops:
  232.5 8.5 copy-start.27
  232.5 8.5 copy-start.23
  233.6 7.5 copy-start.29
  233.6 7.7 copy-start.24
  235.1 15.6 all-to-all-start
  393.1 4.9 copy-start.2
  433.2 4.0 copy-start.10
  536.4 10.2 copy-start.28
  536.4 10.2 copy-start.30
  542.6 13.5 all-to-all-start.1
  573.8 13.6 copy-start.1
  573.8 30.6 %copy-start = (f32[2,64,2048]{2,1,0:T(8,128)S(1)}, f32[2,64,2048]{2,1,0:T(8,128)}, u32[]{:S(2)}) copy-start(f32[2,64,2048]{2,1,0:T(8,128)} %param.20) | copy-start | bytes 3145732
  829.8 24.8 %copy-start.31 = (f32[64]{0:T(128)S(1)}, f32[64]{0:T(128)}, u32[]{:S(2)}) copy-start(f32[64]{0:T(128)} %param.22) | copy-start | bytes 772
  829.8 24.8 %copy-start.32 = (f32[64]{0:T(128)S(1)}, f32[64]{0:T(128)}, u32[]{:S(2)}) copy-start(f32[64]{0:T(128)} %param.21) | copy-start | bytes 772
  832.3 23.8 %all-to-all-start.2 = ((f32[2,2,128,128]{3,1,0,2:T(2,128)}), f32[2,2,128,128]{3,1,0,2:T(2,128)S(1)}, u32[]{:S(2)}, u32[]{:S(2)}) async-start(f32[2,2,128,128]{3,1,0,2:T(2,128)} %copy.735), calls=%async_computation.2 | async-start | bytes 524288 | tf_op jit(solution)/shard_map/all_to_all | solution.py:116
  1000.6 5.0 copy-start.4
  1029.6 4.0 copy-start.17
  1149.5 13.2 all-to-all-start.3
  1451.1 24.1 %all-to-all-start.4 = ((f32[2,2,128,128]{3,1,0,2:T(2,128)}), f32[2,2,128,128]{3,1,0,2:T(2,128)S(1)}, u32[]{:S(2)}, u32[]{:S(2)}) async-start(f32[2,2,128,128]{3,1,0,2:T(2,128)} %copy.783), calls=%async_computation.4 | async-start | bytes 524288 | tf_op jit(solution)/shard_map/all_to_all | solution.py:116
  1619.6 5.0 copy-start.6
  1768.3 13.1 all-to-all-start.5
  1771.7 510.5 %reduce-scatter.2.cloned.1.call-start = ((), (), s32[]{:S(2)}) async-start(), calls=%async_computation.8 | async-start | bytes 1310720 | tf_op jit(solution)/shard_map/reduce_scatter | solution.py:170
  1827.9 7.1 copy-start.25
  2208.7 5.0 copy-start.8
  (16 other events, 53.5 us)
Sparse Core Ops, SparseCore 0:
  2255.5 26.6 reduce-scatter.1
